TPU v7x, 256 devices: a whole 4x4x8 slice. The times are simulated.
256 devices in a mesh: seq: 32 (over z, x), head: 8 (over y, core).
Axes of the slice: x: 4, y: 4, z: 8, core: 2. Of those that a mesh axis runs over, the one named last changes fastest.
Arguments:
- queries: bfloat16 [128, 8192], P('seq', 'head'), may hold values from -15 to 15, as said below
- prefix_keys: bfloat16 [2, 262144, 1024], P(None, 'seq', 'head'), may hold values from -6 to 6, as said below
- prefix_values: bfloat16 [2, 262144, 1024], P(None, 'seq', 'head'), may hold values from -6 to 6
- private_suffix_keys: bfloat16 [128, 1024, 1024], P('seq', None, 'head'), may hold values from -9 to 9
- suffix_values: bfloat16 [128, 1024, 1024], P('seq', None, 'head'), may hold values from -6 to 6
- new_key: bfloat16 [128, 1024], P('seq', 'head'), may hold values from -24 to 24, as said below
- new_value: bfloat16 [128, 1024], P('seq', 'head'), may hold values from -6 to 6
- suffix_lengths: int32 [128], P('seq'), may hold values from 128 to 1024, as said below
- prompt_of: int32 [128], replicated, may hold values from 0 to 1, as said below
- out_weight: bfloat16 [8192, 8192], P('head', 'seq'), may hold values from -0.0625 to 0.0625
Outputs:
- mixed: bfloat16 [128, 8192], P('head', 'seq')
Inputs may be any that keep to these rules, and one draw needn't show every extreme that they name: `queries`: every value lies between the bounds. `prefix_keys`: every value lies between the bounds. `new_key`: every value lies between the bounds. `suffix_lengths`: at least 128; some sample uses all 1024 entries. `prompt_of`: each prompt has exactly 64 samples.
All inputs are finite; a program needn't handle non-finite values.
Results may differ from a plain program's by a relative error of at most 0.022.
Values may be sent and summed in bfloat16 or wider, within the bound.
No kernel may reach another device: no remote copies, remote signals or barrier semaphores. Data moves between devices by JAX's collectives and lax.ppermute only.
A program may use at most 128 MiB of HBM per device.

v0:
```python
import math

import jax
import jax.numpy as jnp
from jax import lax
from jax.experimental import pallas as pl
from jax.experimental.pallas import tpu as pltpu
from jax.sharding import PartitionSpec as P

HEAD_SIZE = 128
NT = (((1,), (1,)), ((), ()))
BLOCK = 2048
TILE = 256
PARTS = 2
EARLY = 4096
PREPARE_LIMIT = 4 * 2**20
PREFIX_LIMIT = 40 * 2**20


def prepare_kernel(
    prompt_ref,
    lengths_ref,
    q_ref,
    new_key_ref,
    new_value_ref,
    suffix_keys_hbm,
    suffix_values_hbm,
    keys_hbm,
    values_hbm,
    keys_ref,
    values_ref,
    place_ref,
    back_ref,
    sums_ref,
    tops_ref,
    totals_ref,
    suffix_keys,
    suffix_values,
    sems,
):
    f32 = jnp.float32
    copies = [
        pltpu.make_async_copy(source, target, sems.at[i])
        for i, (source, target) in enumerate(
            (
                (suffix_keys_hbm, suffix_keys),
                (suffix_values_hbm, suffix_values),
                (keys_hbm.at[0, pl.ds(0, keys_ref.shape[0])], keys_ref),
                (values_hbm.at[0, pl.ds(0, values_ref.shape[0])], values_ref),
            )
        )
    ]
    for copy in copies:
        copy.start()

    samples = prompt_ref.shape[1]
    second = prompt_ref[...] == 1
    row = lax.broadcasted_iota(jnp.int32, (samples, samples), 0)
    column = lax.broadcasted_iota(jnp.int32, (samples, samples), 1)
    upto = (row <= column).astype(jnp.bfloat16)
    flags = jnp.broadcast_to(second.astype(f32), (16, samples)).astype(jnp.bfloat16)
    count = jnp.dot(flags, upto, preferred_element_type=f32)[:1].astype(jnp.int32)
    at = lax.broadcasted_iota(jnp.int32, (1, samples), 1)
    rank = jnp.where(second, samples // 2 + count - 1, at - count)
    place = (row == rank).astype(f32)
    place_ref[...] = place.astype(jnp.bfloat16)
    back_ref[...] = place.T.astype(jnp.bfloat16)

    owned, width = q_ref.shape
    heads = width // HEAD_SIZE
    capacity = suffix_keys.shape[1]
    scale = 1.0 / HEAD_SIZE**0.5
    every_q = q_ref[...].astype(f32)
    new_keys = new_key_ref[...].astype(f32)
    new_values = new_value_ref[...].astype(f32)
    position = lax.broadcasted_iota(jnp.int32, (heads, capacity), 1)
    diagonal = lax.broadcasted_iota(jnp.int32, (heads, HEAD_SIZE), 0) == (
        lax.broadcasted_iota(jnp.int32, (heads, HEAD_SIZE), 1)
    )
    copies[0].wait()
    copies[1].wait()
    all_sums, all_tops, all_totals = [], [], []
    for s in range(owned):
        q = jnp.concatenate(
            [every_q[s : s + 1, h * HEAD_SIZE : (h + 1) * HEAD_SIZE] for h in range(heads)], axis=0
        )
        scores = (
            lax.dot_general(
                q.astype(jnp.bfloat16), suffix_keys[s], NT, preferred_element_type=f32
            )
            * scale
        )
        scores = jnp.where(position < lengths_ref[s], scores, -1e30)
        fresh = jnp.sum(q * new_keys[s : s + 1], axis=1, keepdims=True) * scale
        top = jnp.maximum(jnp.max(scores, axis=1, keepdims=True), fresh)
        weights = jnp.exp(scores - top)
        weight = jnp.exp(fresh - top)
        total = jnp.sum(weights, axis=1, keepdims=True) + weight
        sums = (
            jnp.dot(weights.astype(jnp.bfloat16), suffix_values[s], preferred_element_type=f32)
            + weight.astype(jnp.bfloat16).astype(f32) * new_values[s : s + 1]
        )
        all_sums.append(jnp.concatenate([sums[h : h + 1] for h in range(heads)], axis=1))
        all_tops.append(jnp.sum(jnp.where(diagonal, top, 0.0), axis=0, keepdims=True))
        all_totals.append(jnp.sum(jnp.where(diagonal, total, 0.0), axis=0, keepdims=True))
    tops_ref[...] = jnp.concatenate(all_tops, axis=0)
    totals_ref[...] = jnp.concatenate(all_totals, axis=0)
    sums_ref[...] = jnp.concatenate(all_sums, axis=0)
    copies[2].wait()
    copies[3].wait()


def prepare(
    prompt_of, lengths, q, new_key, new_value, suffix_keys, suffix_values, prefix_keys, prefix_values
):
    samples = prompt_of.shape[0]
    owned, width = q.shape
    heads = width // HEAD_SIZE
    square = pltpu.VMEM((samples, samples), jnp.bfloat16)
    vmem = pl.BlockSpec(memory_space=pltpu.VMEM)
    hbm = pl.BlockSpec(memory_space=pltpu.HBM)
    lines = jax.ShapeDtypeStruct((owned, HEAD_SIZE), jnp.float32)
    large = [
        pltpu.with_memory_space_constraint(x, pltpu.HBM)
        for x in (suffix_keys, suffix_values, prefix_keys, prefix_values)
    ]
    return pl.pallas_call(
        prepare_kernel,
        in_specs=[vmem, pl.BlockSpec(memory_space=pltpu.SMEM), vmem, vmem, vmem] + [hbm] * 4,
        out_specs=[vmem] * 7,
        out_shape=[
            pltpu.VMEM((EARLY, HEAD_SIZE), prefix_keys.dtype),
            pltpu.VMEM((EARLY, HEAD_SIZE), prefix_values.dtype),
            square,
            square,
            jax.ShapeDtypeStruct((owned, width), jnp.float32),
            lines,
            lines,
        ],
        scratch_shapes=[
            pltpu.VMEM(suffix_keys.shape, suffix_keys.dtype),
            pltpu.VMEM(suffix_values.shape, suffix_values.dtype),
            pltpu.SemaphoreType.DMA((4,)),
        ],
        compiler_params=pltpu.CompilerParams(vmem_limit_bytes=PREPARE_LIMIT),
        cost_estimate=pl.CostEstimate(
            flops=4 * owned * suffix_keys.shape[1] * width,
            bytes_accessed=4 * EARLY * HEAD_SIZE + 4 * suffix_keys.size,
            transcendentals=owned * suffix_keys.shape[1] * heads,
        ),
        name="prepare",
    )(prompt_of.reshape(1, samples), lengths, q, new_key, new_value, *large)


def lane_tops(scores):
    tops = scores[:, :HEAD_SIZE]
    for at in range(HEAD_SIZE, scores.shape[1], HEAD_SIZE):
        tops = jnp.maximum(tops, scores[:, at : at + HEAD_SIZE])
    return tops


def prefix_kernel(
    q_ref,
    place_ref,
    back_ref,
    early_keys,
    early_values,
    keys_hbm,
    values_hbm,
    out_ref,
    keys,
    values,
    sorted_q,
    acc,
    top,
    sems,
):
    early = early_keys.shape[0]
    span = keys.shape[1]
    rest = pl.ds(early, span - early)
    copies = [
        [
            pltpu.make_async_copy(keys_hbm.at[0, rest], keys.at[0, rest], sems.at[0]),
            pltpu.make_async_copy(values_hbm.at[0, rest], values.at[0, rest], sems.at[1]),
        ],
        [
            pltpu.make_async_copy(keys_hbm.at[1], keys.at[1], sems.at[2]),
            pltpu.make_async_copy(values_hbm.at[1], values.at[1], sems.at[3]),
        ],
    ]
    for copy in copies[0]:
        copy.start()

    def block_of(start, whole, p, first):
        if p == 0 and first < early:
            return start[first : first + TILE, :]
        return whole[p, first : first + TILE, :]

    samples, width = q_ref.shape
    heads = width // HEAD_SIZE
    per = samples // 2
    rows = per * heads
    part = rows // PARTS
    tiles = BLOCK // TILE
    blocks = span // BLOCK
    f32 = jnp.float32
    scale = math.log2(math.e) / HEAD_SIZE**0.5

    ordered = jnp.dot(place_ref[...], q_ref[...], preferred_element_type=f32) * scale
    for p in range(2):
        for h in range(heads):
            x = ordered[p * per : (p + 1) * per, h * HEAD_SIZE : (h + 1) * HEAD_SIZE]
            high = x.astype(jnp.bfloat16)
            sorted_q[p, h * per : (h + 1) * per, :HEAD_SIZE] = high
            sorted_q[p, h * per : (h + 1) * per, HEAD_SIZE:] = (x - high.astype(f32)).astype(
                jnp.bfloat16
            )

    lane = lax.broadcasted_iota(jnp.int32, (per, HEAD_SIZE), 1)

    def finish(p):
        tops = top[p] * math.log(2.0)
        sent = tops.astype(jnp.bfloat16).astype(f32)
        sums = acc[p] * jnp.exp(tops - sent)
        extra = jnp.zeros((per, HEAD_SIZE), f32)
        pieces = []
        for h in range(heads):
            r = slice(h * per, (h + 1) * per)
            total = sums[r, HEAD_SIZE:]
            high = total.astype(jnp.bfloat16).astype(f32)
            extra = jnp.where(lane == h, sent[r], extra)
            extra = jnp.where(lane == heads + h, high, extra)
            extra = jnp.where(lane == 2 * heads + h, total - high, extra)
            pieces.append(sums[r, :HEAD_SIZE].astype(jnp.bfloat16))
        return jnp.concatenate(pieces + [extra.astype(jnp.bfloat16)], axis=1)

    def score(p, t, r):
        k = block_of(early_keys, keys, p, t * TILE)
        return lax.dot_general(
            sorted_q[p, r * part : (r + 1) * part],
            jnp.concatenate([k, k], axis=1),
            NT,
            preferred_element_type=f32,
        )

    finished = []
    steps = [(p, j) for p in range(2) for j in range(blocks)]
    scores = [[None] * tiles for _ in range(PARTS)]
    peaks = [None] * PARTS
    for t in range(tiles):
        for r in range(PARTS):
            scores[r][t] = score(0, t, r)
            seen = lane_tops(scores[r][t])
            peaks[r] = seen if t == 0 else jnp.maximum(peaks[r], seen)
    for number, (p, j) in enumerate(steps):
        if j == 0:
            tops = [jnp.full((part, 1), -1e30, f32)] * PARTS
            sums = [jnp.zeros((part, 2 * HEAD_SIZE), f32)] * PARTS
        if number == 0:
            for copy in copies[1]:
                copy.start()
        if number == early // BLOCK - 1:
            for copy in copies[0]:
                copy.wait()
        if number == blocks - 1:
            for copy in copies[1]:
                copy.wait()
        following = steps[number + 1] if number + 1 < len(steps) else None
        later = [[None] * tiles for _ in range(PARTS)]
        later_peaks = [None] * PARTS
        for r in range(PARTS):
            risen = jnp.maximum(tops[r], jnp.max(peaks[r], axis=1, keepdims=True))
            sums[r] = sums[r] * jnp.exp2(tops[r] - risen)
            tops[r] = risen
        for t in range(tiles):
            for r in range(PARTS):
                if following is not None:
                    later[r][t] = score(following[0], following[1] * tiles + t, r)
                    seen = lane_tops(later[r][t])
                    later_peaks[r] = seen if t == 0 else jnp.maximum(later_peaks[r], seen)
                weights = jnp.exp2(scores[r][t] - tops[r]).astype(jnp.bfloat16)
                first = j * BLOCK + t * TILE
                v = block_of(early_values, values, p, first)
                sums[r] = sums[r] + jnp.dot(
                    weights,
                    jnp.concatenate([v, jnp.ones_like(v)], axis=1),
                    preferred_element_type=f32,
                )
        scores, peaks = later, later_peaks
        if j == blocks - 1:
            for r in range(PARTS):
                top[p, r * part : (r + 1) * part] = tops[r]
                acc[p, r * part : (r + 1) * part] = sums[r]
            finished.append(finish(p))

    both = jnp.concatenate(finished, axis=0)
    out_ref[...] = jnp.dot(back_ref[...], both, preferred_element_type=f32).astype(jnp.bfloat16)


def prefix(q, place, back, early_keys, early_values, keys, values):
    samples, width = q.shape
    rows = samples // 2 * (width // HEAD_SIZE)
    return pl.pallas_call(
        prefix_kernel,
        in_specs=[pl.BlockSpec(memory_space=pltpu.VMEM)] * 5
        + [pl.BlockSpec(memory_space=pltpu.HBM)] * 2,
        out_specs=pl.BlockSpec(memory_space=pltpu.VMEM),
        out_shape=jax.ShapeDtypeStruct((samples, width + HEAD_SIZE), jnp.bfloat16),
        scratch_shapes=[
            pltpu.VMEM(keys.shape, keys.dtype),
            pltpu.VMEM(values.shape, values.dtype),
            pltpu.VMEM((2, rows, 2 * HEAD_SIZE), jnp.bfloat16),
            pltpu.VMEM((2, rows, 2 * HEAD_SIZE), jnp.float32),
            pltpu.VMEM((2, rows, 1), jnp.float32),
            pltpu.SemaphoreType.DMA((4,)),
        ],
        compiler_params=pltpu.CompilerParams(vmem_limit_bytes=PREFIX_LIMIT),
        name="prefix",
    )(
        q,
        place,
        back,
        pltpu.with_memory_space_constraint(early_keys, pltpu.VMEM),
        pltpu.with_memory_space_constraint(early_values, pltpu.VMEM),
        pltpu.with_memory_space_constraint(keys, pltpu.HBM),
        pltpu.with_memory_space_constraint(values, pltpu.HBM),
    )


def gather(block, axis):
    everyone = jnp.broadcast_to(block[None], (lax.axis_size(axis),) + block.shape)
    return lax.all_to_all(everyone, axis, 0, 0)


def per_device(
    queries,
    prefix_keys,
    prefix_values,
    private_suffix_keys,
    suffix_values,
    new_key,
    new_value,
    suffix_lengths,
    prompt_of,
    out_weight,
):
    owned, width = queries.shape
    heads = width // HEAD_SIZE
    seq = lax.axis_size("seq")
    f32 = jnp.float32

    early_keys, early_values, place, back, own_sums, own_top, own_total = prepare(
        prompt_of,
        suffix_lengths,
        queries,
        new_key,
        new_value,
        private_suffix_keys,
        suffix_values,
        prefix_keys,
        prefix_values,
    )
    own_sums = own_sums.reshape(owned, heads, HEAD_SIZE)
    own_top = own_top[:, :heads]
    own_total = own_total[:, :heads]
    every_query = gather(queries, "seq").reshape(seq * owned, width)
    partial = prefix(
        every_query, place, back, early_keys, early_values, prefix_keys, prefix_values
    )
    got = lax.all_to_all(partial.reshape(seq, owned, width + HEAD_SIZE), "seq", 0, 0)

    got = got.astype(f32)
    sums = got[:, :, :width].reshape(seq, owned, heads, HEAD_SIZE)
    tops = got[:, :, width : width + heads]
    totals = (
        got[:, :, width + heads : width + 2 * heads]
        + got[:, :, width + 2 * heads : width + 3 * heads]
    )
    overall = jnp.maximum(jnp.max(tops, axis=0), own_top)
    factors = jnp.exp(tops - overall)
    own_factor = jnp.exp(own_top - overall)
    total = jnp.sum(totals * factors, axis=0) + own_total * own_factor
    numer = jnp.sum(sums * factors[..., None], axis=0) + own_sums * own_factor[..., None]
    context = (numer / total[..., None]).astype(jnp.bfloat16).reshape(owned, width)

    partial_out = jnp.dot(
        gather(context, "seq").reshape(seq * owned, width), out_weight, preferred_element_type=f32
    ).astype(jnp.bfloat16)
    groups = lax.axis_size("head")
    pieces = lax.all_to_all(partial_out.reshape(groups, -1, partial_out.shape[1]), "head", 0, 0)
    return jnp.sum(pieces.astype(f32), axis=0).astype(jnp.bfloat16)


def solution(mesh):
    placed = (
        P("seq", "head"),
        P(None, "seq", "head"),
        P(None, "seq", "head"),
        P("seq", None, "head"),
        P("seq", None, "head"),
        P("seq", "head"),
        P("seq", "head"),
        P("seq"),
        P(),
        P("head", "seq"),
    )
    return jax.shard_map(
        per_device, mesh=mesh, in_specs=placed, out_specs=P("head", "seq"), check_vma=False
    )
```

profile of v0, /device:TPU:1, one launch (start us, length us, event | category | flops | bytes accessed | tf_op | source)
XLA Modules:
  0.0 81.1 jit_solution(17588516016662434585)
XLA Ops:
  0.0 0.0 copy-start
  0.0 1.5 %broadcast_in_dim.4 = bf16[32,4,1024]{2,1,0:T(4,128)(2,1)} broadcast(bf16[4,1024]{1,0:T(4,128)(2,1)} %q_ref.1), dimensions={1,2} | broadcast | bytes 270336 | tf_op jit(solution)/shard_map/broadcast_in_dim | solution.py:331
  1.5 11.9 %all-to-all-start = ((bf16[32,4,1024]{2,1,0:T(4,128)(2,1)}), bf16[32,4,1024]{2,1,0:T(4,128)(2,1)S(1)}, u32[]{:S(2)}, u32[]{:S(2)}) async-start(bf16[32,4,1024]{2,1,0:T(4,128)(2,1)} %broadcast_in_dim.4), calls=%async_computation | async-start | bytes 524288 | tf_op jit(solution)/shard_map/all_to_all | solution.py:332
  13.4 0.0 copy-start.1
  13.4 0.7 copy-done.1
  14.1 0.0 copy-start.2
  14.1 0.7 copy-done.2
  14.8 0.0 copy-start.3
  14.8 0.7 copy-done.3
  15.5 0.0 copy-start.4
  15.5 0.7 copy-done.4
  16.1 0.0 copy-start.5
  16.1 0.7 copy-done.5
  16.8 3.4 %prepare.1 = (bf16[4096,128]{1,0:T(8,128)(2,1)S(1)}, bf16[4096,128]{1,0:T(8,128)(2,1)S(1)}, bf16[128,128]{1,0:T(8,128)(2,1)S(1)}, bf16[128,128]{1,0:T(8,128)(2,1...) custom-call(s32[1,128]{1,0:T(1,128)S(1)} %bitcast.22, s32[4]{0:T(128)S(1)} %copy-done.5, ...), custom_call_target="tpu_custom_call" | custom-call | flops 16777216 | bytes 4194304 | tf_op jit(solution)/shard_map/prepare/pallas_call | solution.py:127
  20.2 4.4 %all-to-all-done = bf16[32,4,1024]{2,1,0:T(4,128)(2,1)S(1)} async-done(((bf16[32,4,1024]{2,1,0:T(4,128)(2,1)}), bf16[32,4,1024]{2,1,0:T(4,128)(2,1)S(1)}, u32[]{:S(2)}, u32[]{:S(2)}) %all-to-all-start) | async-done | bytes 262176 | tf_op jit(solution)/shard_map/all_to_all | solution.py:332
  24.6 0.1 reshape.40.q_ref
  24.6 10.4 %prefix.1 = bf16[128,1152]{1,0:T(8,128)(2,1)S(1)} custom-call(bf16[128,1024]{1,0:T(8,128)(2,1)S(1)} %reshape.40.q_ref, bf16[128,128]{1,0:T(8,128)(2,1)S(1)} %get-tuple-element.12.place_ref, bf16[128,128]{1,0:T(8,128)(2,1)S(1)} %get-tuple-element.13.back_ref, bf16[4096,128]{1,0:T(8,128)(2,1)S(1)} %get-tuple-element.14.early_keys, ...), custom_call_target="tpu_custom_call" | custom-call | tf_op jit(solution)/shard_map/prefix/pallas_call | solution.py:303
  35.1 0.1 reshape.42
  35.2 15.6 %all_to_all.20 = bf16[32,4,1152]{2,1,0:T(4,128)(2,1)S(1)} all-to-all(bf16[32,4,1152]{2,1,0:T(4,128)(2,1)S(1)} %reshape.42), channel_id=1, replica_groups=mesh['seq'=32,'head'=8] {'seq'}, dimensions={0} | all-to-all | bytes 589824 | tf_op jit(solution)/shard_map/all_to_all | solution.py:370
  50.9 0.1 fusion.2
  51.0 0.2 mul.29
  51.2 0.2 mul.30
  51.4 0.1 fusion
  51.6 0.1 broadcast_bitcast_fusion
  51.7 0.1 broadcast_in_dim.5
  51.7 15.5 %all_to_all.21 = bf16[32,4,1024]{2,1,0:T(4,128)(2,1)S(1)} all-to-all(bf16[32,4,1024]{2,1,0:T(4,128)(2,1)S(1)} %broadcast_in_dim.5), channel_id=1, replica_groups=mesh['seq'=32,'head'=8] {'seq'}, dimensions={0} | all-to-all | bytes 524288 | tf_op jit(solution)/shard_map/all_to_all | solution.py:332
  67.3 0.1 reshape.43
  67.3 0.0 copy-done
  67.3 0.2 convolution_convert_fusion
  67.6 12.9 %all_to_all.22 = bf16[8,16,256]{2,1,0:T(8,128)(2,1)S(1)} all-to-all(bf16[8,16,256]{2,1,0:T(8,128)(2,1)S(1)} %bitcast.23), channel_id=1, replica_groups=mesh['seq'=32,'head'=8] {'head'}, dimensions={0} | all-to-all | bytes 131072 | tf_op jit(solution)/shard_map/all_to_all | solution.py:390
  80.5 0.6 reduce_sum.32
  (5 shorter events, 0.1 us)
Async XLA Ops:
  0.0 67.3 %copy-start = (bf16[1024,256]{1,0:T(8,128)(2,1)S(1)}, bf16[1024,256]{1,0:T(8,128)(2,1)}, u32[]{:S(2)}) copy-start(bf16[1024,256]{1,0:T(8,128)(2,1)} %param.19) | copy-start | bytes 1572868
  1.5 23.1 %all-to-all-start = ((bf16[32,4,1024]{2,1,0:T(4,128)(2,1)}), bf16[32,4,1024]{2,1,0:T(4,128)(2,1)S(1)}, u32[]{:S(2)}, u32[]{:S(2)}) async-start(bf16[32,4,1024]{2,1,0:T(4,128)(2,1)} %broadcast_in_dim.4), calls=%async_computation | async-start | bytes 524288 | tf_op jit(solution)/shard_map/all_to_all | solution.py:332
  13.4 0.7 copy-start.1
  14.1 0.7 copy-start.2
  14.8 0.7 copy-start.3
  15.5 0.7 copy-start.4
  16.1 0.7 copy-start.5
where the time goes:
time: 81.5 us; the launch traced here: 81.1 us
  blocking collectives  44 us (54%)
  Pallas kernels  13.8 us (17%)
  starting transfers between devices  11.9 us (15%)
  local copies, waits for them, and re-layouts  5.6 us (7%)
  waiting for transfers between devices  4.4 us (5%)
  other arithmetic  1.02 us (1%)
    all_to_all x1, blocking collectives, per_device(): lax.all_to_all(partial.reshape(seq, owned, width + HEAD_SIZE), 'seq', 0, 0)  15.6 us
    all_to_all x1, blocking collectives, gather(): return lax.all_to_all(everyone, axis, 0, 0)  15.5 us
    all_to_all x1, blocking collectives, per_device(): lax.all_to_all(partial_out.reshape(groups, -1, partial_out.shape[1]), 'he...  12.9 us
    all_to_all x1, starting transfers between devices, gather(): return lax.all_to_all(everyone, axis, 0, 0)  11.9 us
    pallas_call x1, Pallas kernels, prefix(): pl.pallas_call(prefix_kernel, in_specs=[pl.BlockSpec(memory_space=pltpu.V...  10.4 us
    all_to_all x1, waiting for transfers between devices, gather(): return lax.all_to_all(everyone, axis, 0, 0)  4.4 us
    unnamed x13, local copies, waits for them, and re-layouts  3.44 us
    pallas_call x1, Pallas kernels, prepare(): pl.pallas_call(prepare_kernel, in_specs=[vmem, pl.BlockSpec(memory_space=...  3.4 us
  transfers between devices with their start and end apart: 1, of which 1 were waited for; matrix products, arithmetic and copies ran while one was open for 0% of the time, Pallas kernels for 4%

commit v1 on v0

--- a/solution.py
+++ b/solution.py
@@ -360,7 +360,6 @@
         prefix_keys,
         prefix_values,
     )
-    own_sums = own_sums.reshape(owned, heads, HEAD_SIZE)
     own_top = own_top[:, :heads]
     own_total = own_total[:, :heads]
     every_query = gather(queries, "seq").reshape(seq * owned, width)
@@ -370,7 +369,6 @@
     got = lax.all_to_all(partial.reshape(seq, owned, width + HEAD_SIZE), "seq", 0, 0)
 
     got = got.astype(f32)
-    sums = got[:, :, :width].reshape(seq, owned, heads, HEAD_SIZE)
     tops = got[:, :, width : width + heads]
     totals = (
         got[:, :, width + heads : width + 2 * heads]
@@ -380,8 +378,13 @@
     factors = jnp.exp(tops - overall)
     own_factor = jnp.exp(own_top - overall)
     total = jnp.sum(totals * factors, axis=0) + own_total * own_factor
-    numer = jnp.sum(sums * factors[..., None], axis=0) + own_sums * own_factor[..., None]
-    context = (numer / total[..., None]).astype(jnp.bfloat16).reshape(owned, width)
+    pieces = []
+    for h in range(heads):
+        columns = slice(h * HEAD_SIZE, (h + 1) * HEAD_SIZE)
+        numer = jnp.sum(got[:, :, columns] * factors[:, :, h : h + 1], axis=0)
+        numer = numer + own_sums[:, columns] * own_factor[:, h : h + 1]
+        pieces.append((numer / total[:, h : h + 1]).astype(jnp.bfloat16))
+    context = jnp.concatenate(pieces, axis=1)
 
     partial_out = jnp.dot(
         gather(context, "seq").reshape(seq * owned, width), out_weight, preferred_element_type=f32

time: 81.5 us -> 89.2 us (1.094)
  other arithmetic: 1.02 us -> 6.56 us
  local copies, waits for them, and re-layouts: 5.6 us -> 7.42 us
    unnamed x0 -> x7, other arithmetic: none -> 4.6 us
    slice x0 -> x10, local copies, waits for them, and re-layouts: none -> 1.57 us  [the longest x9 1.13 us: per_device(): numer = jnp.sum(got[:, :, columns] * factors[:, :, h:h + 1], axis=0)]
    unnamed x13 -> x14, local copies, waits for them, and re-layouts: 3.44 us -> 3.37 us
where the time goes in v1:
time: 89.2 us; the launch traced here: 88.6 us
  blocking collectives  44.2 us (50%)
  Pallas kernels  13.8 us (15%)
  starting transfers between devices  11.9 us (13%)
  local copies, waits for them, and re-layouts  7.42 us (8%)
  other arithmetic  6.56 us (7%)
  waiting for transfers between devices  4.39 us (5%)
    all_to_all x1, blocking collectives, per_device(): lax.all_to_all(partial.reshape(seq, owned, width + HEAD_SIZE), 'seq', 0, 0)  15.8 us
    all_to_all x1, blocking collectives, gather(): return lax.all_to_all(everyone, axis, 0, 0)  15.5 us
    all_to_all x1, blocking collectives, per_device(): lax.all_to_all(partial_out.reshape(groups, -1, partial_out.shape[1]), 'he...  12.9 us
    all_to_all x1, starting transfers between devices, gather(): return lax.all_to_all(everyone, axis, 0, 0)  11.9 us
    pallas_call x1, Pallas kernels, prefix(): pl.pallas_call(prefix_kernel, in_specs=[pl.BlockSpec(memory_space=pltpu.V...  10.4 us
    unnamed x7, other arithmetic  4.6 us
    all_to_all x1, waiting for transfers between devices, gather(): return lax.all_to_all(everyone, axis, 0, 0)  4.39 us
    pallas_call x1, Pallas kernels, prepare(): pl.pallas_call(prepare_kernel, in_specs=[vmem, pl.BlockSpec(memory_space=...  3.4 us
  transfers between devices with their start and end apart: 1, of which 1 were waited for; matrix products, arithmetic and copies ran while one was open for 0% of the time, Pallas kernels for 4%

profile of v1, /device:TPU:1, one launch (start us, length us, event | category | flops | bytes accessed | tf_op | source)
XLA Modules:
  0.0 88.6 jit_solution(15442989360627360212)
XLA Ops:
  0.0 1.5 %broadcast_in_dim.4 = bf16[32,4,1024]{2,1,0:T(4,128)(2,1)} broadcast(bf16[4,1024]{1,0:T(4,128)(2,1)} %q_ref.1), dimensions={1,2} | broadcast | bytes 270336 | tf_op jit(solution)/shard_map/broadcast_in_dim | solution.py:331
  1.5 11.9 %all-to-all-start = ((bf16[32,4,1024]{2,1,0:T(4,128)(2,1)}), bf16[32,4,1024]{2,1,0:T(4,128)(2,1)S(1)}, u32[]{:S(2)}, u32[]{:S(2)}) async-start(bf16[32,4,1024]{2,1,0:T(4,128)(2,1)} %broadcast_in_dim.4), calls=%async_computation | async-start | bytes 524288 | tf_op jit(solution)/shard_map/all_to_all | solution.py:332
  13.4 0.0 copy-start.1
  13.4 0.7 copy-done.1
  14.1 0.7 copy-done.3
  14.8 0.7 copy-done.4
  15.5 0.7 copy-done.5
  16.1 0.7 copy-done.6
  16.8 3.4 %prepare.1 = (bf16[4096,128]{1,0:T(8,128)(2,1)S(1)}, bf16[4096,128]{1,0:T(8,128)(2,1)S(1)}, bf16[128,128]{1,0:T(8,128)(2,1)S(1)}, bf16[128,128]{1,0:T(8,128)(2,1...) custom-call(s32[1,128]{1,0:T(1,128)S(1)} %bitcast.12, s32[4]{0:T(128)S(1)} %copy-done.6, ...), custom_call_target="tpu_custom_call" | custom-call | flops 16777216 | bytes 4194304 | tf_op jit(solution)/shard_map/prepare/pallas_call | solution.py:127
  20.2 4.4 %all-to-all-done = bf16[32,4,1024]{2,1,0:T(4,128)(2,1)S(1)} async-done(((bf16[32,4,1024]{2,1,0:T(4,128)(2,1)}), bf16[32,4,1024]{2,1,0:T(4,128)(2,1)S(1)}, u32[]{:S(2)}, u32[]{:S(2)}) %all-to-all-start) | async-done | bytes 262176 | tf_op jit(solution)/shard_map/all_to_all | solution.py:332
  24.6 0.1 reshape.18.q_ref
  24.6 10.4 %prefix.1 = bf16[128,1152]{1,0:T(8,128)(2,1)S(1)} custom-call(bf16[128,1024]{1,0:T(8,128)(2,1)S(1)} %reshape.18.q_ref, bf16[128,128]{1,0:T(8,128)(2,1)S(1)} %get-tuple-element.12.place_ref, bf16[128,128]{1,0:T(8,128)(2,1)S(1)} %get-tuple-element.13.back_ref, bf16[4096,128]{1,0:T(8,128)(2,1)S(1)} %get-tuple-element.14.early_keys, ...), custom_call_target="tpu_custom_call" | custom-call | tf_op jit(solution)/shard_map/prefix/pallas_call | solution.py:303
  35.1 0.1 reshape.20
  35.2 15.8 %all_to_all.20 = bf16[32,4,1152]{2,1,0:T(4,128)(2,1)S(1)} all-to-all(bf16[32,4,1152]{2,1,0:T(4,128)(2,1)S(1)} %reshape.20), channel_id=1, replica_groups=mesh['seq'=32,'head'=8] {'seq'}, dimensions={0} | all-to-all | bytes 589824 | tf_op jit(solution)/shard_map/all_to_all | solution.py:369
  51.0 0.1 fusion.8
  51.2 0.3 fusion.18
  51.5 0.1 copy.17
  51.6 0.1 copy.43
  51.7 0.1 copy.39
  51.8 0.1 copy.35
  51.9 0.1 copy.31
  52.0 0.1 copy.27
  52.1 0.1 copy.23
  52.2 0.1 copy.47
  52.3 0.1 copy.48
  52.4 0.1 copy.24
  52.5 0.1 copy.28
  52.6 0.1 copy.32
  52.7 0.1 copy.36
  52.8 0.1 copy.40
  52.9 0.1 copy.44
  52.9 0.1 copy.18
  53.0 0.4 slice_reduce_fusion.1
  53.5 0.3 fusion
  53.9 0.1 constant_dynamic-update-slice_fusion.7
  53.9 0.8 constant_dynamic-update-slice_fusion.6
  54.7 0.7 constant_dynamic-update-slice_fusion.5
  55.4 0.8 constant_dynamic-update-slice_fusion.4
  56.2 0.8 constant_dynamic-update-slice_fusion.3
  56.9 0.8 constant_dynamic-update-slice_fusion.2
  57.7 0.8 constant_dynamic-update-slice_fusion.1
  58.5 0.8 constant_dynamic-update-slice_fusion
  59.2 0.1 broadcast_in_dim.5
  59.3 15.5 %all_to_all.21 = bf16[32,4,1024]{2,1,0:T(4,128)(2,1)S(1)} all-to-all(bf16[32,4,1024]{2,1,0:T(4,128)(2,1)S(1)} %broadcast_in_dim.5), channel_id=1, replica_groups=mesh['seq'=32,'head'=8] {'seq'}, dimensions={0} | all-to-all | bytes 524288 | tf_op jit(solution)/shard_map/all_to_all | solution.py:332
  74.8 0.1 reshape.21
  74.9 0.2 convolution_convert_fusion
  75.1 12.9 %all_to_all.22 = bf16[8,16,256]{2,1,0:T(8,128)(2,1)S(1)} all-to-all(bf16[8,16,256]{2,1,0:T(8,128)(2,1)S(1)} %bitcast.13), channel_id=1, replica_groups=mesh['seq'=32,'head'=8] {'head'}, dimensions={0} | all-to-all | bytes 131072 | tf_op jit(solution)/shard_map/all_to_all | solution.py:393
  88.0 0.6 reduce_sum.102
  (12 shorter events, 0.1 us)
Async XLA Ops:
  0.0 74.9 %copy-start = (bf16[1024,256]{1,0:T(8,128)(2,1)S(1)}, bf16[1024,256]{1,0:T(8,128)(2,1)}, u32[]{:S(2)}) copy-start(bf16[1024,256]{1,0:T(8,128)(2,1)} %param.19) | copy-start | bytes 1572868
  1.5 23.1 %all-to-all-start = ((bf16[32,4,1024]{2,1,0:T(4,128)(2,1)}), bf16[32,4,1024]{2,1,0:T(4,128)(2,1)S(1)}, u32[]{:S(2)}, u32[]{:S(2)}) async-start(bf16[32,4,1024]{2,1,0:T(4,128)(2,1)} %broadcast_in_dim.4), calls=%async_computation | async-start | bytes 524288 | tf_op jit(solution)/shard_map/all_to_all | solution.py:332
  13.4 0.7 copy-start.1
  14.1 0.7 copy-start.3
  14.8 0.7 copy-start.4
  15.5 0.7 copy-start.5
  16.1 0.7 copy-start.6
  20.2 33.7 %copy-start.2 = (f32[4,1024]{1,0:T(4,128)}, f32[4,1024]{1,0:T(4,128)S(1)}, u32[]{:S(2)}) copy-start(f32[4,1024]{1,0:T(4,128)S(1)} %get-tuple-element.17) | copy-start | bytes 49156
